TPU v7x, 512 devices: a whole 4x8x8 slice. The times are simulated.
512 devices in a mesh: team: 32 (over x_lo, z, core), member: 16 (over x_hi, y).
Axes of the slice: x: 4 (x_hi: 2, x_lo: 2; x = x_hi * 2 + x_lo), y: 8, z: 8, core: 2. Of those that a mesh axis runs over, the one named last changes fastest.
Arguments:
- feats: bfloat16 [65536, 128], P(('team', 'member')), may hold values from -6 to 6
- tile_weights: bfloat16 [32, 16, 16, 8, 128, 128], P('team', 'member'), may hold values from -6 to 6
- tile_rows: int32 [32, 16, 16, 8], P('team', 'member'), may hold values from 0 to 31, as said below
- slot_count: int32 [32, 16, 16], P('team', 'member'), may hold values from 1 to 8, as said below
- degrees: int32 [65536], P(('member', 'team')), may hold values from 2048 to 8192
- weight: bfloat16 [128, 256], replicated, may hold values from -0.5 to 0.5
- grad_out: bfloat16 [65536, 256], P(('member', 'team')), may hold values from -6 to 6
Outputs:
- out: bfloat16 [65536, 256], P(('member', 'team'))
- grad_weight: float32 [128, 256], replicated
- grad_feats: float32 [65536, 128], P(('team', 'member'))
Inputs may be any that keep to these rules, and one draw needn't show every extreme that they name: `tile_rows`: within one column block of one device the 8 entries are distinct row blocks. `slot_count`: every device has a column block with all 8 slots live.
All inputs are finite; a program needn't handle non-finite values.
Results may differ from a plain program's by a relative error of at most 0.0049.
Values may be sent and summed in bfloat16 or wider, within the bound.
A program may use at most 64 MiB of HBM per device.

v0:
```python
import jax
import jax.numpy as jnp
from jax import lax
from jax.sharding import PartitionSpec as P


def scale_rows(cotangent, inv_scale, weight):
    projected = lax.dot_general(
        cotangent, weight, (((1,), (1,)), ((), ())), preferred_element_type=jnp.float32
    )
    return (projected * inv_scale[:, None]).astype(jnp.bfloat16)


def per_device(feats, tile_weights, tile_rows, slot_count, degrees, weight, grad_out):
    tiles = tile_weights[0, 0]
    row_ids = tile_rows[0, 0]
    counts = slot_count[0, 0]
    col_blocks, slot_num = row_ids.shape
    tile_size = tiles.shape[-1]
    feat_width = feats.shape[1]
    row_blocks = lax.axis_size("team") * feats.shape[0] // tile_size
    live_mask = jnp.arange(slot_num, dtype=jnp.int32)[None, :] < counts[:, None]
    live_scale = live_mask.astype(jnp.float32)
    zero_rows = jnp.zeros((row_blocks, tile_size, feat_width), jnp.float32)
    team_feats = lax.all_gather(feats, "member", axis=0, tiled=True)
    block_count = team_feats.shape[0] // tile_size
    x_blocks = team_feats.reshape(block_count, tile_size, feat_width)

    def add_column(offset, running):
        column = 0 + offset
        tile_vals = lax.dynamic_index_in_dim(tiles, column, 0, keepdims=False)
        x_block = lax.dynamic_index_in_dim(x_blocks, offset, 0, keepdims=False)
        products = jnp.einsum("sij,jf->sif", tile_vals, x_block, preferred_element_type=jnp.float32)
        slot_mask = lax.dynamic_index_in_dim(live_scale, column, 0, keepdims=False)
        targets = lax.dynamic_index_in_dim(row_ids, column, 0, keepdims=False)
        return running.at[targets].add(products * slot_mask[:, None, None])

    partial_value = lax.fori_loop(0, block_count, add_column, zero_rows)
    summed = lax.psum_scatter(
        partial_value.reshape(row_blocks * tile_size, feat_width),
        "team",
        scatter_dimension=0,
        tiled=True,
    )
    inv_root = lax.rsqrt(degrees.astype(jnp.float32))
    aggregate = (summed * inv_root[:, None]).astype(jnp.bfloat16)
    out = jnp.dot(aggregate, weight, preferred_element_type=jnp.float32).astype(jnp.bfloat16)
    local_grad = lax.dot_general(
        aggregate, grad_out, (((0,), (0,)), ((), ())), preferred_element_type=jnp.float32
    )
    node_total = feats.shape[0] * lax.axis_size("team") * lax.axis_size("member")
    grad_weight = lax.psum(local_grad, ("team", "member")) * node_total ** (-0.5)
    team_grad, team_deg = (
        lax.all_gather(grad_out, "team", axis=0, tiled=True),
        lax.all_gather(degrees, "team", axis=0, tiled=True),
    )
    team_scaled = scale_rows(team_grad, lax.rsqrt(team_deg.astype(jnp.float32)), weight)
    scaled_blocks = team_scaled.reshape(row_blocks, tile_size, feat_width)

    def column_sum(column):
        tile_vals = tiles[column]
        picked = scaled_blocks[row_ids[column]]
        picked = jnp.where(live_mask[column][:, None, None], picked, jnp.zeros((), jnp.bfloat16))
        return jnp.einsum("sji,sjf->if", tile_vals, picked, preferred_element_type=jnp.float32)

    col_partial = lax.map(column_sum, jnp.arange(col_blocks, dtype=jnp.int32))
    grad_feats = lax.psum_scatter(
        col_partial.reshape(col_blocks * tile_size, feat_width),
        "member",
        scatter_dimension=0,
        tiled=True,
    )
    return (out, grad_weight, grad_feats)


def solution(mesh):
    placed = (
        P(("team", "member"), None),
        P("team", "member", None, None, None, None),
        P("team", "member", None, None),
        P("team", "member", None),
        P(("member", "team")),
        P(),
        P(("member", "team"), None),
    )
    return jax.shard_map(
        per_device,
        mesh=mesh,
        in_specs=placed,
        out_specs=(P(("member", "team"), None), P(), P(("team", "member"), None)),
        check_vma=False,
    )
```

profile of v0, /device:TPU:1, one launch (start us, length us, event | category | flops | bytes accessed | tf_op | source)
XLA Modules:
  0.0 680.3 jit_solution(10209551838707623828)
XLA Ops:
  9.4 38.1 %all_gather.9 = bf16[2048,128]{1,0:T(8,128)(2,1)S(1)} all-gather(bf16[128,128]{1,0:T(8,128)(2,1)} %param.11), channel_id=1, replica_groups=mesh['team'=32,'member'=16] {'member'}, dimensions={0}, use_global_device_ids=true | all-gather | bytes 557056 | tf_op jit(solution)/shard_map/all_gather | solution.py:25
  47.8 36.3 %while.23 = (s32[]{:T(128)}, f32[32,128,128]{2,1,0:T(8,128)S(1)}, s32[16,8]{1,0:T(8,128)S(1)}, bf16[16,8,128,128]{3,2,1,0:T(8,128)(2,1)}, bf16[16,128,128]{2,1,0...) while((s32[]{:T(128)}, f32[32,128,128]{2,1,0:T(8,128)S(1)}, s32[16,8]{1,0:T(8,128)S(1)}, ...), condition=%wide.region_2.3_spmd, body=%wide.region_0.2_spmd.sunk | while | flops 33816600 | bytes 2393845 | solution.py:38
  85.5 6.4 copy.14
  91.9 47.2 %all-gather = s32[32,1,128]{2,1,0:T(1,128)S(1)} all-gather(s32[1,1,128]{2,1,0:T(1,128)S(1)} %bitcast.84), channel_id=1, replica_groups=mesh['team'=32,'member'=16] {'team'}, dimensions={0}, use_global_device_ids=true | all-gather | bytes 16896 | tf_op jit(solution)/shard_map/all_gather | solution.py:55
  139.2 2.3 fusion.18
  141.5 67.5 %reduce-scatter.3.cloned.1.call-done = f32[128,128]{1,0:T(8,128)} async-done(((f32[4096,128]{1,0:T(8,128)}), f32[128,128]{1,0:T(8,128)}) %reduce-scatter.3.cloned.1.call-update) | async-done | bytes 65552 | tf_op jit(solution)/shard_map/reduce_scatter | solution.py:39
  210.9 80.9 %while.24 = (s32[]{:T(128)}, f32[16,128,128]{2,1,0:T(8,128)}, s32[16]{0:T(128)S(1)}, bf16[16,8,128,128]{2,3,1,0:T(8,128)(2,1)}, pred[16,8]{1,0:T(8,128)(4,1)S(1)...) while((s32[]{:T(128)}, f32[16,128,128]{2,1,0:T(8,128)}, ...), condition=%wide.region_6.7_spmd, body=%wide.region_5.6_spmd.sunk | while | flops 33686556 | bytes 1119031 | solution.py:66
  214.1 1.9 fusion.40
  219.1 1.9 fusion.40
  224.2 1.9 fusion.40
  229.2 1.9 fusion.40
  234.3 1.9 fusion.40
  239.4 1.9 fusion.40
  244.4 1.9 fusion.40
  249.5 1.9 fusion.40
  254.5 1.9 fusion.40
  259.6 1.9 fusion.40
  264.7 1.9 fusion.40
  269.7 1.9 fusion.40
  274.8 1.9 fusion.40
  284.9 1.9 fusion.40
  290.0 1.9 fusion.40
  292.7 183.7 %all-reduce.2.cloned.1.call-done = f32[128,256]{1,0:T(8,128)} async-done(((f32[128,256]{1,0:T(8,128)}), f32[128,256]{1,0:T(8,128)}) %all-reduce.2.cloned.1.call-update) | async-done | bytes 131088 | tf_op jit(solution)/shard_map/psum | solution.py:52
  478.0 195.8 %reduce-scatter.5.cloned.1.call-done = f32[128,128]{1,0:T(8,128)} async-done(((f32[2048,128]{1,0:T(8,128)}), f32[128,128]{1,0:T(8,128)}) %reduce-scatter.5.cloned.1.call-update) | async-done | bytes 65552 | tf_op jit(solution)/shard_map/reduce_scatter | solution.py:67
  (174 shorter events, 65.0 us)
Async XLA Ops:
  7.2 132.0 %copy-start = (bf16[128,256]{1,0:T(8,128)(2,1)S(1)}, bf16[128,256]{1,0:T(8,128)(2,1)}, u32[]{:S(2)}) copy-start(bf16[128,256]{1,0:T(8,128)(2,1)} %param.16) | copy-start | bytes 196612
  7.2 132.0 %all-gather.3.cloned.1.call-start = ((), (), s32[]{:S(2)}) async-start(), calls=%async_computation.4 | async-start | bytes 2162688 | tf_op jit(solution)/shard_map/all_gather | solution.py:54
  7.9 201.1 %reduce-scatter.3.cloned.1.call-start = ((), (), s32[]{:S(2)}) async-start(), calls=%async_computation.2 | async-start | bytes 2162688 | tf_op jit(solution)/shard_map/reduce_scatter | solution.py:39
  84.1 1.4 copy-start.1
  85.5 6.5 copy-start.4
  85.5 390.9 %all-reduce.2.cloned.1.call-start = ((), (), s32[]{:S(2)}) async-start(), calls=%async_computation.3 | async-start | bytes 262144 | tf_op jit(solution)/shard_map/psum | solution.py:52
  91.9 117.1 %copy-start.3 = (bf16[128,256]{1,0:T(8,128)(2,1)S(1)}, bf16[128,256]{1,0:T(8,128)(2,1)}, u32[]{:S(2)}) copy-start(bf16[128,256]{1,0:T(8,128)(2,1)} %param.17) | copy-start | bytes 196612
  210.8 463.0 %reduce-scatter.5.cloned.1.call-start = ((), (), s32[]{:S(2)}) async-start(), calls=%async_computation.5 | async-start | bytes 1114112 | tf_op jit(solution)/shard_map/reduce_scatter | solution.py:67
  210.9 81.0 %copy-start.2 = (f32[128,128]{1,0:T(8,128)S(1)}, f32[128,128]{1,0:T(8,128)}, u32[]{:S(2)}) copy-start(f32[128,128]{1,0:T(8,128)} %reduce-scatter.3.cloned.1.call-done) | copy-start | bytes 196612
Sparse Core Ops, SparseCore 0:
  10.2 73.7 all-gather.2
  86.8 122.2 reduce-scatter.2
  215.4 260.9 all-reduce.1
  481.2 192.5 reduce-scatter.4
where the time goes:
time: 686 us; the launch traced here: 680 us
  waiting for transfers between devices  448 us (65%)
  blocking collectives  85.3 us (12%)
  matrix products  53.6 us (8%)
  loops' own time  32.3 us (5%)
  local copies, waits for them, and re-layouts  28 us (4%)
  other arithmetic  19.4 us (3%)
  between operations  13.9 us (2%)
    reduce_scatter x1, waiting for transfers between devices, per_device(): lax.psum_scatter(col_partial.reshape(col_blocks * tile_size, feat_width),...  196 us
    psum x1, waiting for transfers between devices, per_device(): lax.psum(local_grad, ('team', 'member')) * node_total ** (-0.5)  184 us
    reduce_scatter x1, waiting for transfers between devices, per_device(): lax.psum_scatter(partial_value.reshape(row_blocks * tile_size, feat_width...  67.5 us
    all_gather x1, blocking collectives, per_device(): lax.all_gather(degrees, 'team', axis=0, tiled=True)  47.2 us
    all_gather x1, blocking collectives, per_device(): team_feats = lax.all_gather(feats, 'member', axis=0, tiled=True)  38.1 us
    another operation x1, loops' own time, per_device(): col_partial = lax.map(column_sum, jnp.arange(col_blocks, dtype=jnp.int32))  31.6 us
    dot_general x16, matrix products, column_sum(): jnp.einsum('sji,sjf->if', tile_vals, picked, preferred_element_type=jnp.f...  30 us
    dot_general x16, matrix products, add_column(): jnp.einsum('sij,jf->sif', tile_vals, x_block, preferred_element_type=jnp....  18.7 us
  transfers between devices with their start and end apart: 4, of which 3 were waited for; matrix products, arithmetic and copies ran while one was open for 14% of the time, Pallas kernels for 0%

commit v1 on v0

v1 whole, which is shorter than its diff:
```python
import jax
import jax.numpy as jnp
from jax import lax
from jax.experimental import pallas as pl
from jax.experimental.pallas import tpu as pltpu
from jax.sharding import PartitionSpec as P

MESH = pl.DeviceIdType.MESH
F32 = jnp.float32
BF16 = jnp.bfloat16

N_TEAM, N_MEMBER, N_CHIP = 32, 16, 16
BLOCK, FEAT, HID, SLOTS = 128, 128, 256, 8
COLS = 16
DEAD = COLS * SLOTS
SLAB = BLOCK // 8


def kernel(slot_of, row_of, feats, tiles_hbm, degrees, weight, grad_out,
           out, grad_weight, grad_feats,
           tiles, x_all, s_all, prod, from_sib, to_sib, own_part, to_team, from_team,
           to_member, from_member, gw_part, slab_in, slab, y_in, slab_y, z_in,
           tile_sem, x_send, x_recv, s_send, s_recv, f_send, f_recv, cs_send, cs_recv,
           t_send, t_recv, b_send, b_recv, g_send, g_recv, y_send, y_recv, z_send, z_recv,
           a_send, a_recv):
    t = lax.axis_index("team")
    m = lax.axis_index("member")
    core = lax.rem(t, 2)
    chip = t // 2
    z = lax.rem(chip, 8)
    x_lo = chip // 8
    y = lax.rem(m, 8)
    x_hi = m // 8
    sib = chip * 2 + 1 - core
    group = core + 2 * x_lo + 4 * x_hi

    def copy(src, dst, send, recv, team, member):
        return pltpu.make_async_remote_copy(
            src_ref=src, dst_ref=dst, send_sem=send, recv_sem=recv,
            device_id=(team, member), device_id_type=MESH)

    def member_peer(k):
        return lax.rem(m + k, N_MEMBER)

    def chip_peer(k):
        return lax.rem(chip + k, N_CHIP)

    def flip(j):
        c = 1 - core if j & 1 else core
        xl = 1 - x_lo if j & 2 else x_lo
        xh = 1 - x_hi if j & 4 else x_hi
        return (xl * 8 + z) * 2 + c, xh * 8 + y, c + 2 * xl + 4 * xh

    def tile_copy(c):
        return pltpu.make_async_copy(tiles_hbm.at[c], tiles.at[c], tile_sem.at[c])

    for c in range(COLS):
        tile_copy(c).start()

    barrier = pltpu.get_barrier_semaphore()

    @pl.loop(1, N_MEMBER)
    def _(k):
        pl.semaphore_signal(barrier, inc=1, device_id=(t, member_peer(k)), device_id_type=MESH)

    @pl.loop(1, N_CHIP)
    def _(k):
        pl.semaphore_signal(barrier, inc=1, device_id=(chip_peer(k) * 2 + core, m), device_id_type=MESH)

    pl.semaphore_signal(barrier, inc=1, device_id=(sib, m), device_id_type=MESH)
    for j in (3, 5, 6, 7):
        to_t, to_m, _ = flip(j)
        pl.semaphore_signal(barrier, inc=1, device_id=(to_t, to_m), device_id_type=MESH)

    inv_row = lax.rsqrt(degrees[...].astype(F32))
    scaled_t = lax.dot_general(weight[...], grad_out[...], (((1,), (1,)), ((), ())),
                               preferred_element_type=F32)
    s_all[t] = (scaled_t * inv_row).astype(BF16)
    s_all[N_TEAM] = jnp.zeros((FEAT, BLOCK), BF16)
    x_all[m] = feats[...]
    prod[DEAD] = jnp.zeros((BLOCK, FEAT), F32)
    inv_col = jnp.transpose(jnp.broadcast_to(inv_row, (BLOCK, BLOCK)))

    pl.semaphore_wait(barrier, 2 * 15 + 5)

    def x_copy(k):
        return copy(feats, x_all.at[m], x_send.at[k], x_recv.at[k], t, member_peer(k))

    def s_copy(k):
        return copy(s_all.at[t], s_all.at[t], s_send.at[k], s_recv.at[k], chip_peer(k) * 2 + core, m)

    def forward_copy(k):
        src = lax.rem(chip - k + N_CHIP, N_CHIP) * 2 + core
        return copy(s_all.at[src], s_all.at[src], f_send.at[k], f_recv.at[k], sib, m)

    forward_copy(0).start()

    @pl.loop(1, N_MEMBER)
    def _(k):
        x_copy(k).start()
        s_copy(k).start()

    for c in range(COLS):
        tile_copy(c).wait()

    def multiply(c):
        products = jnp.dot(tiles[c], x_all[c], preferred_element_type=F32)
        prod[pl.ds(c * SLOTS, SLOTS)] = products.reshape(SLOTS, BLOCK, FEAT)

    multiply(m)

    @pl.loop(1, N_MEMBER)
    def _(k):
        x_copy(k).wait_recv()
        multiply(lax.rem(m - k + N_MEMBER, N_MEMBER))
        s_copy(k).wait_recv()
        forward_copy(k).start()

    def row_sum(r):
        total = prod[slot_of[0, r]]
        for c in range(1, COLS):
            total = total + prod[slot_of[c, r]]
        return total

    def cs_copy(q):
        return copy(to_sib.at[q], from_sib.at[q], cs_send.at[q], cs_recv.at[q], sib, m)

    def t_copy(k):
        return copy(to_team.at[k], from_team.at[k], t_send.at[k], t_recv.at[k],
                    chip_peer(k) * 2 + core, m)

    @pl.loop(1, N_CHIP + 1)
    def _(k):
        q = chip_peer(k)
        to_sib[q] = row_sum(q * 2 + 1 - core).astype(BF16)
        cs_copy(q).start()

    @pl.loop(1, N_CHIP)
    def _(k):
        q = chip_peer(k)
        mine = row_sum(q * 2 + core)
        cs_copy(q).wait_recv()
        to_team[k] = (mine + from_sib[q].astype(F32)).astype(BF16)
        t_copy(k).start()

    mine = row_sum(t)
    cs_copy(chip).wait_recv()
    own_part[...] = mine + from_sib[chip].astype(F32)

    @pl.loop(0, N_CHIP)
    def _(k):
        src = lax.rem(chip - k + N_CHIP, N_CHIP) * 2 + 1 - core
        copy(s_all.at[src], s_all.at[src], f_send.at[k], f_recv.at[k], sib, m).wait_recv()

    def column(c):
        picked = jnp.concatenate([s_all[row_of[c, s]] for s in range(SLOTS)], axis=1)
        return jnp.dot(picked, tiles[c], preferred_element_type=F32)

    def b_copy(k):
        return copy(to_member.at[k], from_member.at[k], b_send.at[k], b_recv.at[k], t, member_peer(k))

    @pl.loop(1, N_MEMBER)
    def _(k):
        to_member[k] = column(member_peer(k)).astype(BF16)
        b_copy(k).start()

    own_col = column(m)

    @pl.loop(1, N_CHIP)
    def _(k):
        t_copy(k).wait_recv()

    summed = own_part[...]
    for k in range(1, N_CHIP):
        summed = summed + from_team[k].astype(F32)
    aggregate = (summed * inv_col).astype(BF16)
    gw_part[...] = lax.dot_general(aggregate, grad_out[...], (((0,), (0,)), ((), ())),
                                   preferred_element_type=F32).reshape(8, SLAB, HID)

    def g_copy(j):
        to_t, to_m, to_g = flip(j)
        return copy(gw_part.at[to_g], slab_in.at[j], g_send.at[j], g_recv.at[j], to_t, to_m)

    for j in range(1, 8):
        g_copy(j).start()

    out[...] = jnp.dot(aggregate, weight[...], preferred_element_type=F32).astype(BF16)

    for j in range(1, 8):
        g_copy(j).wait_recv()
    part = gw_part[group]
    for j in range(1, 8):
        part = part + slab_in[j]
    slab[...] = part

    def y_copy(k):
        return copy(slab, y_in.at[k], y_send.at[k], y_recv.at[k], t, x_hi * 8 + lax.rem(y + k, 8))

    def z_copy(k):
        return copy(slab_y, z_in.at[k], z_send.at[k], z_recv.at[k],
                    (x_lo * 8 + lax.rem(z + k, 8)) * 2 + core, m)

    for k in range(1, 8):
        y_copy(k).start()

    @pl.loop(1, N_MEMBER)
    def _(k):
        b_copy(k).wait_recv()

    for k in range(1, N_MEMBER):
        own_col = own_col + from_member[k].astype(F32)
    grad_feats[...] = jnp.transpose(own_col)

    for k in range(1, 8):
        y_copy(k).wait_recv()
    part = slab[...]
    for k in range(1, 8):
        part = part + y_in[k]
    slab_y[...] = part
    for k in range(1, 8):
        z_copy(k).start()
    for k in range(1, 8):
        z_copy(k).wait_recv()
    part = slab_y[...]
    for k in range(1, 8):
        part = part + z_in[k]
    grad_weight[group] = part * (N_TEAM * N_MEMBER * BLOCK) ** (-0.5)

    def a_copy(j):
        to_t, to_m, _ = flip(j)
        return copy(grad_weight.at[group], grad_weight.at[group], a_send.at[j], a_recv.at[j], to_t, to_m)

    for j in range(1, 8):
        a_copy(j).start()

    @pl.loop(1, N_MEMBER)
    def _(k):
        x_copy(k).wait_send()
        s_copy(k).wait_send()
        t_copy(k).wait_send()
        b_copy(k).wait_send()

    @pl.loop(0, N_CHIP)
    def _(k):
        forward_copy(k).wait_send()
        cs_copy(k).wait_send()

    for j in range(1, 8):
        g_copy(j).wait_send()
        y_copy(j).wait_send()
        z_copy(j).wait_send()
        a_copy(j).wait_send()
    for j in range(1, 8):
        a_copy(j).wait_recv()


def per_device(feats, tile_weights, tile_rows, slot_count, degrees, weight, grad_out):
    rows = tile_rows[0, 0]
    live = jnp.arange(SLOTS, dtype=jnp.int32)[None, :] < slot_count[0, 0][:, None]
    row_of = jnp.where(live, rows, N_TEAM)
    slot_ids = jnp.arange(COLS * SLOTS, dtype=jnp.int32).reshape(COLS, SLOTS)
    hit = row_of[:, None, :] == jnp.arange(N_TEAM, dtype=jnp.int32)[None, :, None]
    slot_of = jnp.min(jnp.where(hit, slot_ids[:, None, :], DEAD), axis=2)

    smem = pl.BlockSpec(memory_space=pltpu.SMEM)
    vmem = pl.BlockSpec(memory_space=pltpu.VMEM)
    hbm = pl.BlockSpec(memory_space=pl.ANY)
    dma = pltpu.SemaphoreType.DMA
    block = (BLOCK, FEAT)
    out, grad_weight, grad_feats = pl.pallas_call(
        kernel,
        out_shape=(
            jax.ShapeDtypeStruct((BLOCK, HID), BF16),
            jax.ShapeDtypeStruct((8, SLAB, HID), F32),
            jax.ShapeDtypeStruct((BLOCK, FEAT), F32),
        ),
        in_specs=[smem, smem, vmem, hbm, vmem, vmem, vmem],
        out_specs=(vmem, vmem, vmem),
        scratch_shapes=[
            pltpu.VMEM((COLS, SLOTS * BLOCK, BLOCK), BF16),
            pltpu.VMEM((COLS,) + block, BF16),
            pltpu.VMEM((N_TEAM + 1,) + block, BF16),
            pltpu.VMEM((DEAD + 1,) + block, F32),
            pltpu.VMEM((N_CHIP,) + block, BF16),
            pltpu.VMEM((N_CHIP,) + block, BF16),
            pltpu.VMEM(block, F32),
            pltpu.VMEM((N_CHIP,) + block, BF16),
            pltpu.VMEM((N_CHIP,) + block, BF16),
            pltpu.VMEM((N_MEMBER,) + block, BF16),
            pltpu.VMEM((N_MEMBER,) + block, BF16),
            pltpu.VMEM((8, SLAB, HID), F32),
            pltpu.VMEM((8, SLAB, HID), F32),
            pltpu.VMEM((SLAB, HID), F32),
            pltpu.VMEM((8, SLAB, HID), F32),
            pltpu.VMEM((SLAB, HID), F32),
            pltpu.VMEM((8, SLAB, HID), F32),
            dma((COLS,)),
            dma((16,)), dma((16,)), dma((16,)), dma((16,)), dma((16,)), dma((16,)), dma((16,)), dma((16,)),
            dma((16,)), dma((16,)), dma((16,)), dma((16,)), dma((8,)), dma((8,)), dma((8,)), dma((8,)),
            dma((8,)), dma((8,)), dma((8,)), dma((8,)),
        ],
        compiler_params=pltpu.CompilerParams(
            collective_id=0, has_side_effects=True, vmem_limit_bytes=62 * 1024 * 1024),
    )(
        slot_of, row_of, feats,
        tile_weights.reshape(COLS, SLOTS * BLOCK, BLOCK),
        degrees.reshape(1, BLOCK), weight, grad_out,
    )
    return out, grad_weight.reshape(BLOCK, HID), grad_feats


def solution(mesh):
    placed = (
        P(("team", "member"), None),
        P("team", "member", None, None, None, None),
        P("team", "member", None, None),
        P("team", "member", None),
        P(("member", "team")),
        P(),
        P(("member", "team"), None),
    )
    return jax.shard_map(
        per_device,
        mesh=mesh,
        in_specs=placed,
        out_specs=(P(("member", "team"), None), P(), P(("team", "member"), None)),
        check_vma=False,
    )
```

time: 686 us -> 80 us (0.12)
  waiting for transfers between devices: 448 us -> 0 us
  blocking collectives: 85.3 us -> 0 us
  Pallas kernels: 0 us -> 72.3 us
  matrix products: 53.6 us -> 0 us
  loops' own time: 32.3 us -> 0 us
  local copies, waits for them, and re-layouts: 28 us -> 5.27 us
  other arithmetic: 19.4 us -> 1.44 us
  between operations: 13.9 us -> 0.64 us
    reduce_scatter x2 -> x0, waiting for transfers between devices: 263 us -> none  [the longest x1 196 us: per_device(): lax.psum_scatter(col_partial.reshape(col_blocks * tile_size, feat_width),...]
    psum x1 -> x0, waiting for transfers between devices: 184 us -> none  [per_device(): lax.psum(local_grad, ('team', 'member')) * node_total ** (-0.5)]
    all_gather x2 -> x0, blocking collectives: 85.3 us -> none  [the longest x1 47.2 us: per_device(): lax.all_gather(degrees, 'team', axis=0, tiled=True)]
    pallas_call x0 -> x1, Pallas kernels: none -> 72.3 us  [per_device(): pl.pallas_call(kernel, out_shape=(jax.ShapeDtypeStruct((BLOCK, HID), BF16...]
    dot_general x35 -> x0, matrix products: 53.6 us -> none  [the longest x16 30 us: column_sum(): jnp.einsum('sji,sjf->if', tile_vals, picked, preferred_element_type=jnp.f...]
    another operation x2 -> x0, loops' own time: 32.3 us -> none  [the longest x1 31.6 us: per_device(): col_partial = lax.map(column_sum, jnp.arange(col_blocks, dtype=jnp.int32))]
    scatter-add x16 -> x0, other arithmetic: 16.6 us -> none  [add_column(): return running.at[targets].add(products * slot_mask[:, None, None])]
    gather x16 -> x0, local copies, waits for them, and re-layouts: 9.56 us -> none  [column_sum(): picked = scaled_blocks[row_ids[column]]]
  transfers between devices with their start and end apart: 4 -> 0, of which waited for: 3 -> 0; matrix products, arithmetic and copies ran while one was open for 14% -> 0% of each run, Pallas kernels for 0% -> 0%
where the time goes in v1:
time: 80 us; the launch traced here: 79.6 us
  Pallas kernels  72.3 us (90%)
  local copies, waits for them, and re-layouts  5.27 us (7%)
  other arithmetic  1.44 us (2%)
    pallas_call x1, Pallas kernels, per_device(): pl.pallas_call(kernel, out_shape=(jax.ShapeDtypeStruct((BLOCK, HID), BF16...  72.3 us
    unnamed x5, local copies, waits for them, and re-layouts  4.52 us

profile of v1, /device:TPU:1, one launch (start us, length us, event | category | flops | bytes accessed | tf_op | source)
XLA Modules:
  0.0 79.6 jit_solution(10637775276949804556)
XLA Ops:
  0.6 0.8 copy.11
  1.4 0.7 multiply_add_fusion
  2.1 0.0 copy-start
  2.1 0.7 select_reduce_fusion.slot_of
  2.8 0.0 copy-done
  2.8 72.3 %shard_map.94 = (bf16[128,256]{1,0:T(8,128)(2,1)}, f32[8,16,256]{2,1,0:T(8,128)}, f32[128,128]{1,0:T(8,128)}) custom-call(s32[16,32]{1,0:T(8,128)} %select_reduce_fusion.slot_of, s32[16,8]{1,0:T(8,128)} %copy-done, bf16[128,128]{1,0:T(8,128)(2,1)} %feats.1, bf16[16,1024,128]{2,1,0:T(8,128)(2,1)} %bitcast.5, s32[1,128]{1,0:T(1,128)} %bitcast.8, ...), custom_call_target="tpu_custom_call" | custom-call | tf_op jit(solution)/shard_map/pallas_call | solution.py:270
  75.1 1.5 %copy.15 = bf16[128,256]{1,0:T(8,128)(2,1)} copy(bf16[128,256]{1,0:T(8,128)(2,1)} %get-tuple-element.14) | data formatting | bytes 131072
  76.6 1.6 %copy.16 = f32[128,256]{1,0:T(8,128)} copy(f32[128,256]{1,0:T(8,128)} %bitcast.6) | data formatting | bytes 262144
  78.2 1.5 %copy.17 = f32[128,128]{1,0:T(8,128)} copy(f32[128,128]{1,0:T(8,128)} %get-tuple-element.16) | data formatting | bytes 131072
Async XLA Ops:
  2.1 0.7 copy-start

commit v2 on v1

v2 whole, which is shorter than its diff:
```python
import jax
import jax.numpy as jnp
from jax import lax
from jax.experimental import pallas as pl
from jax.experimental.pallas import tpu as pltpu
from jax.sharding import PartitionSpec as P

MESH = pl.DeviceIdType.MESH
F32 = jnp.float32
BF16 = jnp.bfloat16

N_TEAM, N_MEMBER, N_CHIP, RING = 32, 16, 16, 8
BLOCK, FEAT, HID, SLOTS = 128, 128, 256, 8
COLS = 16
HELD = SLOTS + 1
SLAB = BLOCK // 8
FAR, NEAR = (4, 3, 5), (6, 2, 7, 1)


def kernel(row_hbm, count_hbm, feats_hbm, tiles_hbm, degrees_hbm, weight_hbm, grad_out_hbm,
           out, grad_weight, grad_feats,
           slot_of, row_of, count, slot_vec, row_vec, count_vec, degrees, weight, grad_out,
           tiles, x_all, s_all, prod, from_sib, to_sib, own_part, to_team, from_team,
           to_member, from_member, gw_part, slab_out, slab_in, slab, y_in, slab_y, z_in,
           in_sem, slot_sem, tile_sem, x_send, x_recv, x2_send, x2_recv, s_send, s_recv, s2_send, s2_recv,
           f_send, f_recv, cs_send, cs_recv,
           t_send, t_recv, b_send, b_recv, g_send, g_recv, y_send, y_recv, z_send, z_recv,
           a_send, a_recv):
    t = lax.axis_index("team")
    m = lax.axis_index("member")
    core = lax.rem(t, 2)
    chip = t // 2
    z = lax.rem(chip, RING)
    x_lo = chip // RING
    y = lax.rem(m, RING)
    x_hi = m // RING
    sib = chip * 2 + 1 - core
    group = core + 2 * x_lo + 4 * x_hi

    def signal(team, member):
        pl.semaphore_signal(barrier, inc=1, device_id=(team, member), device_id_type=MESH)

    def copy(src, dst, send, recv, team, member):
        return pltpu.make_async_remote_copy(
            src_ref=src, dst_ref=dst, send_sem=send, recv_sem=recv,
            device_id=(team, member), device_id_type=MESH)

    def member_peer(k):
        return lax.rem(m + k, N_MEMBER)

    def chip_peer(k):
        return lax.rem(chip + k, N_CHIP)

    def flip(j):
        c = 1 - core if j & 1 else core
        xl = 1 - x_lo if j & 2 else x_lo
        xh = 1 - x_hi if j & 4 else x_hi
        return (xl * RING + z) * 2 + c, xh * RING + y, c + 2 * xl + 4 * xh

    def y_at(k):
        return lax.rem(y + k, RING)

    def z_at(k):
        return lax.rem(z + k, RING)

    def tile_copy(c):
        return pltpu.make_async_copy(tiles_hbm.at[c], tiles.at[c], tile_sem.at[c])

    pairs = ((weight_hbm, weight), (grad_out_hbm, grad_out), (degrees_hbm, degrees),
             (row_hbm, row_vec), (count_hbm, count_vec), (feats_hbm, x_all.at[m]),
             (row_hbm, row_of), (count_hbm, count))
    inputs = [pltpu.make_async_copy(src, dst, in_sem.at[i]) for i, (src, dst) in enumerate(pairs)]
    slot_copy = pltpu.make_async_copy(slot_vec, slot_of, slot_sem)

    barrier = pltpu.get_barrier_semaphore()

    @pl.loop(1, N_MEMBER)
    def _(k):
        signal(t, member_peer(k))
        signal(chip_peer(k) * 2 + core, m)

    signal(sib, m)
    for j in (3, 5, 6, 7):
        to_t, to_m, _ = flip(j)
        signal(to_t, to_m)

    for c in inputs:
        c.start()
    for c in range(COLS):
        tile_copy(c).start()

    pl.semaphore_wait(barrier, 2 * 15 + 5)

    def x_slot(row, k):
        return row * RING + lax.rem(y - k + RING, RING)

    def x_copy(k):
        return copy(feats_hbm, x_all.at[m], x_send.at[k], x_recv.at[k], t, x_hi * RING + y_at(k))

    def x_swap():
        return copy(feats_hbm, x_all.at[m], x2_send.at[0], x2_recv.at[0], t, (1 - x_hi) * RING + y)

    def x_near(k):
        slot = x_slot(1 - x_hi, 0)
        return copy(x_all.at[slot], x_all.at[slot], x2_send.at[k], x2_recv.at[k], t, x_hi * RING + y_at(k))

    def x_far(k):
        slot = x_slot(x_hi, k)
        return copy(x_all.at[slot], x_all.at[slot], x2_send.at[k], x2_recv.at[k], t, (1 - x_hi) * RING + y)

    def s_slot(row, k):
        return (row * RING + lax.rem(z - k + RING, RING)) * 2 + core

    def s_copy(k):
        return copy(s_all.at[t], s_all.at[t], s_send.at[k], s_recv.at[k], (x_lo * RING + z_at(k)) * 2 + core, m)

    def s_swap():
        return copy(s_all.at[t], s_all.at[t], s2_send.at[0], s2_recv.at[0], ((1 - x_lo) * RING + z) * 2 + core, m)

    def s_near(k):
        slot = s_slot(1 - x_lo, 0)
        return copy(s_all.at[slot], s_all.at[slot], s2_send.at[k], s2_recv.at[k],
                    (x_lo * RING + z_at(k)) * 2 + core, m)

    def s_far(k):
        slot = s_slot(x_lo, k)
        return copy(s_all.at[slot], s_all.at[slot], s2_send.at[k], s2_recv.at[k],
                    ((1 - x_lo) * RING + z) * 2 + core, m)

    def pass_on(row, k):
        slot = s_slot(x_lo if row == 0 else 1 - x_lo, k)
        return copy(s_all.at[slot], s_all.at[slot], f_send.at[row * RING + k], f_recv.at[row * RING + k], sib, m)

    def passed(row, k):
        slot = s_slot(x_lo if row == 0 else 1 - x_lo, k) + 1 - 2 * core
        return copy(s_all.at[slot], s_all.at[slot], f_send.at[row * RING + k], f_recv.at[row * RING + k], sib, m)

    x_swap().start()
    for k in FAR + NEAR:
        x_copy(k).start()

    for c in inputs[:3]:
        c.wait()
    inv_row = lax.rsqrt(degrees[...].astype(F32))
    scaled_t = lax.dot_general(weight[...], grad_out[...], (((1,), (1,)), ((), ())),
                               preferred_element_type=F32)
    s_all[t] = (scaled_t * inv_row).astype(BF16)
    s_swap().start()
    for k in FAR + NEAR:
        s_copy(k).start()
    pass_on(0, 0).start()

    for c in inputs[3:]:
        c.wait()
    row_ids = lax.broadcasted_iota(jnp.int32, (N_TEAM, COLS), 0)
    slots = jnp.full((N_TEAM, COLS), SLOTS, jnp.int32)
    for s in range(SLOTS):
        slots = jnp.where((row_vec[s:s + 1, :] == row_ids) & (s < count_vec[...]), s, slots)
    slot_vec[...] = slots
    slot_copy.start()

    s_all[N_TEAM] = jnp.zeros((FEAT, BLOCK), BF16)
    for c in range(COLS):
        prod[c * HELD + SLOTS] = jnp.zeros((BLOCK, FEAT), F32)
    inv_col = jnp.transpose(jnp.broadcast_to(inv_row, (BLOCK, BLOCK)))
    for c in range(COLS):
        tile_copy(c).wait()
    slot_copy.wait()

    def multiply(c):
        products = jnp.dot(tiles[c], x_all[c], preferred_element_type=F32)
        prod[pl.ds(c * HELD, SLOTS)] = products.reshape(SLOTS, BLOCK, FEAT)

    x_swap().wait_recv()
    for k in NEAR:
        x_near(k).start()
    s_swap().wait_recv()
    for k in NEAR:
        s_near(k).start()
    pass_on(1, 0).start()
    multiply(m)
    multiply(x_slot(1 - x_hi, 0))
    for k in FAR:
        x_copy(k).wait_recv()
        x_far(k).start()
        s_copy(k).wait_recv()
        s_far(k).start()
        pass_on(0, k).start()
    for k in FAR:
        multiply(x_slot(x_hi, k))
    for k in NEAR:
        x_copy(k).wait_recv()
        multiply(x_slot(x_hi, k))
    for k in NEAR:
        s_copy(k).wait_recv()
        pass_on(0, k).start()
    for k in NEAR:
        x_near(k).wait_recv()
        multiply(x_slot(1 - x_hi, k))
    for k in FAR:
        x_far(k).wait_recv()
        multiply(x_slot(1 - x_hi, k))

    def row_sum(r):
        total = prod[slot_of[r, 0]]
        for c in range(1, COLS):
            total = total + prod[c * HELD + slot_of[r, c]]
        return total

    def outward(i):
        return lax.rem(4 + ((i + 1) // 2) * (1 - 2 * lax.rem(i, 2)) + RING, RING)

    def cs_copy(q):
        return copy(to_sib.at[q], from_sib.at[q], cs_send.at[q], cs_recv.at[q], sib, m)

    def t_copy(k):
        return copy(to_team.at[k], from_team.at[k], t_send.at[k], t_recv.at[k],
                    chip_peer(k) * 2 + core, m)

    def for_sibling(q):
        to_sib[q] = row_sum(q * 2 + 1 - core).astype(BF16)
        cs_copy(q).start()

    def for_team(q):
        mine = row_sum(q * 2 + core)
        cs_copy(q).wait_recv()
        k = lax.rem(q - chip + N_CHIP, N_CHIP)
        to_team[k] = (mine + from_sib[q].astype(F32)).astype(BF16)
        t_copy(k).start()

    @pl.loop(0, RING)
    def _(i):
        dz = z_at(outward(i))
        for_sibling((1 - x_lo) * RING + dz)
        for_sibling(x_lo * RING + dz)

    @pl.loop(0, RING - 1)
    def _(i):
        dz = z_at(outward(i))
        for_team((1 - x_lo) * RING + dz)
        for_team(x_lo * RING + dz)

    for_team((1 - x_lo) * RING + z)
    mine = row_sum(t)
    cs_copy(chip).wait_recv()
    own_part[...] = mine + from_sib[chip].astype(F32)

    for k in NEAR:
        s_near(k).wait_recv()
        pass_on(1, k).start()
    for k in FAR:
        s_far(k).wait_recv()
        pass_on(1, k).start()

    @pl.loop(0, RING)
    def _(k):
        passed(0, k).wait_recv()
        passed(1, k).wait_recv()

    def column(c):
        picked = [s_all[jnp.where(s < count[0, c], row_of[s, c], N_TEAM)] for s in range(SLOTS)]
        return jnp.dot(jnp.concatenate(picked, axis=1), tiles[c], preferred_element_type=F32)

    def b_copy(k):
        return copy(to_member.at[k], from_member.at[k], b_send.at[k], b_recv.at[k], t, member_peer(k))

    def for_member(c):
        k = lax.rem(c - m + N_MEMBER, N_MEMBER)
        to_member[k] = column(c).astype(BF16)
        b_copy(k).start()

    @pl.loop(0, RING - 1)
    def _(i):
        dy = y_at(outward(i))
        for_member((1 - x_hi) * RING + dy)
        for_member(x_hi * RING + dy)

    for_member((1 - x_hi) * RING + y)
    own_col = column(m)

    @pl.loop(1, N_CHIP)
    def _(k):
        t_copy(k).wait_recv()

    summed = own_part[...]
    for k in range(1, N_CHIP):
        summed = summed + from_team[k].astype(F32)
    aggregate = (summed * inv_col).astype(BF16)
    part = lax.dot_general(aggregate, grad_out[...], (((0,), (0,)), ((), ())),
                           preferred_element_type=F32).reshape(8, SLAB, HID)
    gw_part[...] = part
    slab_out[...] = part.astype(BF16)

    def g_copy(j):
        to_t, to_m, to_g = flip(j)
        return copy(slab_out.at[to_g], slab_in.at[j], g_send.at[j], g_recv.at[j], to_t, to_m)

    for j in (7, 6, 5, 4, 3, 2, 1):
        g_copy(j).start()

    out[...] = jnp.dot(aggregate, weight[...], preferred_element_type=F32).astype(BF16)

    for j in range(1, 8):
        g_copy(j).wait_recv()
    part = gw_part[group]
    for j in range(1, 8):
        part = part + slab_in[j].astype(F32)
    slab[...] = part.astype(BF16)

    def y_copy(k):
        return copy(slab, y_in.at[k], y_send.at[k], y_recv.at[k], t, x_hi * RING + y_at(k))

    def z_copy(k):
        return copy(slab_y, z_in.at[k], z_send.at[k], z_recv.at[k], (x_lo * RING + z_at(k)) * 2 + core, m)

    for k in FAR + NEAR:
        y_copy(k).start()

    @pl.loop(1, N_MEMBER)
    def _(k):
        b_copy(k).wait_recv()

    for k in range(1, N_MEMBER):
        own_col = own_col + from_member[k].astype(F32)
    grad_feats[...] = jnp.transpose(own_col)

    for k in range(1, RING):
        y_copy(k).wait_recv()
    for k in range(1, RING):
        part = part + y_in[k].astype(F32)
    slab_y[...] = part.astype(BF16)
    for k in FAR + NEAR:
        z_copy(k).start()
    for k in range(1, RING):
        z_copy(k).wait_recv()
    part = slab_y[...].astype(F32)
    for k in range(1, RING):
        part = part + z_in[k].astype(F32)
    grad_weight[group] = part * (N_TEAM * N_MEMBER * BLOCK) ** (-0.5)

    def a_copy(j):
        to_t, to_m, _ = flip(j)
        return copy(grad_weight.at[group], grad_weight.at[group], a_send.at[j], a_recv.at[j], to_t, to_m)

    for j in (7, 6, 5, 4, 3, 2, 1):
        a_copy(j).start()

    @pl.loop(1, N_MEMBER)
    def _(k):
        t_copy(k).wait_send()
        b_copy(k).wait_send()

    @pl.loop(0, N_CHIP)
    def _(k):
        cs_copy(k).wait_send()

    @pl.loop(1, RING)
    def _(k):
        x_copy(k).wait_send()
        s_copy(k).wait_send()

    x_swap().wait_send()
    s_swap().wait_send()
    for k in NEAR:
        x_near(k).wait_send()
        s_near(k).wait_send()
    for k in FAR:
        x_far(k).wait_send()
        s_far(k).wait_send()

    @pl.loop(0, RING)
    def _(k):
        pass_on(0, k).wait_send()
        pass_on(1, k).wait_send()

    for j in range(1, 8):
        g_copy(j).wait_send()
        y_copy(j).wait_send()
        z_copy(j).wait_send()
        a_copy(j).wait_send()
    for j in range(1, 8):
        a_copy(j).wait_recv()


def place(out, grad_weight, grad_feats, to_out, to_weight, to_feats, held_out, held_weight, held_feats, sem):
    held = (held_out, held_weight, held_feats)
    inward = [pltpu.make_async_copy(src, dst, sem.at[i]) for i, (src, dst) in enumerate(zip((out, grad_weight, grad_feats), held))]
    outward = [pltpu.make_async_copy(src, dst, sem.at[i]) for i, (src, dst) in enumerate(zip(held, (to_out, to_weight, to_feats)))]
    for c in inward:
        c.start()
    for c, d in zip(inward, outward):
        c.wait()
        d.start()
    for d in outward:
        d.wait()


def per_device(feats, tile_weights, tile_rows, slot_count, degrees, weight, grad_out):
    rows = tile_rows[0, 0].T
    count = slot_count.reshape(1, COLS)
    vmem = pl.BlockSpec(memory_space=pltpu.VMEM)
    hbm = pl.BlockSpec(memory_space=pl.ANY)
    dma = pltpu.SemaphoreType.DMA
    block = (BLOCK, FEAT)
    out_shape = (
        jax.ShapeDtypeStruct((BLOCK, HID), BF16),
        jax.ShapeDtypeStruct((8, SLAB, HID), F32),
        jax.ShapeDtypeStruct((BLOCK, FEAT), F32),
    )
    results = pl.pallas_call(
        kernel,
        out_shape=out_shape,
        in_specs=[hbm] * 7,
        out_specs=(vmem, vmem, vmem),
        scratch_shapes=[
            pltpu.SMEM((N_TEAM, COLS), jnp.int32),
            pltpu.SMEM((SLOTS, COLS), jnp.int32),
            pltpu.SMEM((1, COLS), jnp.int32),
            pltpu.VMEM((N_TEAM, COLS), jnp.int32),
            pltpu.VMEM((SLOTS, COLS), jnp.int32),
            pltpu.VMEM((1, COLS), jnp.int32),
            pltpu.VMEM((1, BLOCK), jnp.int32),
            pltpu.VMEM((FEAT, HID), BF16),
            pltpu.VMEM((BLOCK, HID), BF16),
            pltpu.VMEM((COLS, SLOTS * BLOCK, BLOCK), BF16),
            pltpu.VMEM((COLS,) + block, BF16),
            pltpu.VMEM((N_TEAM + 1,) + block, BF16),
            pltpu.VMEM((COLS * HELD,) + block, F32),
            pltpu.VMEM((N_CHIP,) + block, BF16),
            pltpu.VMEM((N_CHIP,) + block, BF16),
            pltpu.VMEM(block, F32),
            pltpu.VMEM((N_CHIP,) + block, BF16),
            pltpu.VMEM((N_CHIP,) + block, BF16),
            pltpu.VMEM((N_MEMBER,) + block, BF16),
            pltpu.VMEM((N_MEMBER,) + block, BF16),
            pltpu.VMEM((8, SLAB, HID), F32),
            pltpu.VMEM((8, SLAB, HID), BF16),
            pltpu.VMEM((8, SLAB, HID), BF16),
            pltpu.VMEM((SLAB, HID), BF16),
            pltpu.VMEM((8, SLAB, HID), BF16),
            pltpu.VMEM((SLAB, HID), BF16),
            pltpu.VMEM((8, SLAB, HID), BF16),
            dma((8,)), dma, dma((COLS,)),
            dma((8,)), dma((8,)), dma((8,)), dma((8,)), dma((8,)), dma((8,)), dma((8,)), dma((8,)),
            dma((16,)), dma((16,)), dma((16,)), dma((16,)),
            dma((16,)), dma((16,)), dma((16,)), dma((16,)), dma((8,)), dma((8,)), dma((8,)), dma((8,)),
            dma((8,)), dma((8,)), dma((8,)), dma((8,)),
        ],
        compiler_params=pltpu.CompilerParams(
            collective_id=0, has_side_effects=True, vmem_limit_bytes=60 * 1024 * 1024),
    )(
        rows, count, feats,
        tile_weights.reshape(COLS, SLOTS * BLOCK, BLOCK),
        degrees.reshape(1, BLOCK), weight, grad_out,
    )
    out, grad_weight, grad_feats = pl.pallas_call(
        place,
        out_shape=out_shape,
        in_specs=[hbm] * 3,
        out_specs=(hbm,) * 3,
        scratch_shapes=[pltpu.VMEM(o.shape, o.dtype) for o in out_shape] + [dma((3,))],
    )(*results)
    return out, grad_weight.reshape(BLOCK, HID), grad_feats


def solution(mesh):
    placed = (
        P(("team", "member"), None),
        P("team", "member", None, None, None, None),
        P("team", "member", None, None),
        P("team", "member", None),
        P(("member", "team")),
        P(),
        P(("member", "team"), None),
    )
    return jax.shard_map(
        per_device,
        mesh=mesh,
        in_specs=placed,
        out_specs=(P(("member", "team"), None), P(), P(("team", "member"), None)),
        check_vma=False,
    )
```

time: 80 us -> 66.1 us (0.83)
  Pallas kernels: 72.3 us -> 65.3 us
  local copies, waits for them, and re-layouts: 5.27 us -> 0 us
  other arithmetic: 1.44 us -> 0 us
    pallas_call x1 -> x2, Pallas kernels: 72.3 us -> 65.3 us  [the longest x1 63.7 us: per_device(): pl.pallas_call(kernel, out_shape=out_shape, in_specs=[hbm] * 7, out_specs...]
    unnamed x5 -> x0, local copies, waits for them, and re-layouts: 4.52 us -> none
where the time goes in v2:
time: 66.1 us; the launch traced here: 66 us
  Pallas kernels  65.3 us (99%)
    pallas_call x1, Pallas kernels, per_device(): pl.pallas_call(kernel, out_shape=out_shape, in_specs=[hbm] * 7, out_specs...  63.7 us
    pallas_call x1, Pallas kernels, per_device(): pl.pallas_call(place, out_shape=out_shape, in_specs=[hbm] * 3, out_specs=...  1.64 us

profile of v2, /device:TPU:1, one launch (start us, length us, event | category | flops | bytes accessed | tf_op | source)
XLA Modules:
  0.0 66.0 jit_solution(15294066110417156500)
XLA Ops:
  0.6 63.7 %shard_map.94 = (bf16[128,256]{1,0:T(8,128)(2,1)}, f32[8,16,256]{2,1,0:T(8,128)}, f32[128,128]{1,0:T(8,128)}) custom-call(s32[8,16]{1,0:T(8,128)} %bitcast.8, s32[1,16]{1,0:T(1,128)} %bitcast.9, bf16[128,128]{1,0:T(8,128)(2,1)} %feats_hbm.1, bf16[16,1024,128]{2,1,0:T(8,128)(2,1)} %bitcast.7, s32[1,128]{1,0:T(1,128)} %bitcast.10, ...), custom_call_target="tpu_custom_call" | custom-call | tf_op jit(solution)/shard_map/pallas_call | solution.py:410
  64.3 1.6 %shard_map.95 = (bf16[128,256]{1,0:T(8,128)(2,1)}, f32[8,16,256]{2,1,0:T(8,128)}, f32[128,128]{1,0:T(8,128)}) custom-call(bf16[128,256]{1,0:T(8,128)(2,1)} %get-tuple-element.9.out, f32[8,16,256]{2,1,0:T(8,128)} %get-tuple-element.10.grad_weight, f32[128,128]{1,0:T(8,128)} %get-tuple-element.11.grad_feats), custom_call_target="tpu_custom_call" | custom-call | tf_op jit(solution)/shard_map/pallas_call | solution.py:456

commit v3 on v2

--- a/solution.py
+++ b/solution.py
@@ -15,16 +15,17 @@
 HELD = SLOTS + 1
 SLAB = BLOCK // 8
 FAR, NEAR = (4, 3, 5), (6, 2, 7, 1)
+SPLIT = 4
 
 
 def kernel(row_hbm, count_hbm, feats_hbm, tiles_hbm, degrees_hbm, weight_hbm, grad_out_hbm,
            out, grad_weight, grad_feats,
-           slot_of, row_of, count, slot_vec, row_vec, count_vec, degrees, weight, grad_out,
+           slot_of, row_of, count, slot_vec, row_vec, count_vec, deg_all, weight, g_all, q_t,
            tiles, x_all, s_all, prod, from_sib, to_sib, own_part, to_team, from_team,
-           to_member, from_member, gw_part, slab_out, slab_in, slab, y_in, slab_y, z_in,
-           in_sem, slot_sem, tile_sem, x_send, x_recv, x2_send, x2_recv, s_send, s_recv, s2_send, s2_recv,
+           to_bx, from_bx, held_b, to_member, from_member, gw_part, slab_out, slab_in, slab, y_in, slab_y, z_in,
+           in_sem, slot_sem, tile_sem, x_send, x_recv, x2_send, x2_recv, c_send, c_recv, c2_send, c2_recv, d_send, d_recv,
            f_send, f_recv, cs_send, cs_recv,
-           t_send, t_recv, b_send, b_recv, g_send, g_recv, y_send, y_recv, z_send, z_recv,
+           t_send, t_recv, bx_send, bx_recv, b_send, b_recv, g_send, g_recv, y_send, y_recv, z_send, z_recv,
            a_send, a_recv):
     t = lax.axis_index("team")
     m = lax.axis_index("member")
@@ -45,9 +46,6 @@
             src_ref=src, dst_ref=dst, send_sem=send, recv_sem=recv,
             device_id=(team, member), device_id_type=MESH)
 
-    def member_peer(k):
-        return lax.rem(m + k, N_MEMBER)
-
     def chip_peer(k):
         return lax.rem(chip + k, N_CHIP)
 
@@ -64,9 +62,10 @@
         return lax.rem(z + k, RING)
 
     def tile_copy(c):
-        return pltpu.make_async_copy(tiles_hbm.at[c], tiles.at[c], tile_sem.at[c])
-
-    pairs = ((weight_hbm, weight), (grad_out_hbm, grad_out), (degrees_hbm, degrees),
+        part = pl.ds(c * 4, 4)
+        return pltpu.make_async_copy(tiles_hbm.at[part], tiles.at[part], tile_sem.at[c])
+
+    pairs = ((weight_hbm, weight), (grad_out_hbm, g_all.at[chip]), (degrees_hbm, deg_all.at[chip]),
              (row_hbm, row_vec), (count_hbm, count_vec), (feats_hbm, x_all.at[m]),
              (row_hbm, row_of), (count_hbm, count))
     inputs = [pltpu.make_async_copy(src, dst, in_sem.at[i]) for i, (src, dst) in enumerate(pairs)]
@@ -74,9 +73,12 @@
 
     barrier = pltpu.get_barrier_semaphore()
 
-    @pl.loop(1, N_MEMBER)
-    def _(k):
-        signal(t, member_peer(k))
+    for k in FAR + NEAR:
+        signal(t, x_hi * RING + y_at(k))
+    signal(t, (1 - x_hi) * RING + y)
+
+    @pl.loop(1, N_CHIP)
+    def _(k):
         signal(chip_peer(k) * 2 + core, m)
 
     signal(sib, m)
@@ -84,12 +86,7 @@
         to_t, to_m, _ = flip(j)
         signal(to_t, to_m)
 
-    for c in inputs:
-        c.start()
-    for c in range(COLS):
-        tile_copy(c).start()
-
-    pl.semaphore_wait(barrier, 2 * 15 + 5)
+    pl.semaphore_wait(barrier, RING + N_CHIP - 1 + 5)
 
     def x_slot(row, k):
         return row * RING + lax.rem(y - k + RING, RING)
@@ -108,49 +105,66 @@
         slot = x_slot(x_hi, k)
         return copy(x_all.at[slot], x_all.at[slot], x2_send.at[k], x2_recv.at[k], t, (1 - x_hi) * RING + y)
 
-    def s_slot(row, k):
-        return (row * RING + lax.rem(z - k + RING, RING)) * 2 + core
-
-    def s_copy(k):
-        return copy(s_all.at[t], s_all.at[t], s_send.at[k], s_recv.at[k], (x_lo * RING + z_at(k)) * 2 + core, m)
-
-    def s_swap():
-        return copy(s_all.at[t], s_all.at[t], s2_send.at[0], s2_recv.at[0], ((1 - x_lo) * RING + z) * 2 + core, m)
-
-    def s_near(k):
-        slot = s_slot(1 - x_lo, 0)
-        return copy(s_all.at[slot], s_all.at[slot], s2_send.at[k], s2_recv.at[k],
+    def c_slot(row, k):
+        return row * RING + lax.rem(z - k + RING, RING)
+
+    def c_copy(k):
+        return copy(grad_out_hbm, g_all.at[chip], c_send.at[k], c_recv.at[k], (x_lo * RING + z_at(k)) * 2 + core, m)
+
+    def c_relay(k):
+        back, to = {3: (2, 1), 4: (2, 2), 5: (6, 7)}[k]
+        slot = c_slot(x_lo, back)
+        return copy(g_all.at[slot], g_all.at[slot], c_send.at[k], c_recv.at[k],
+                    (x_lo * RING + z_at(to)) * 2 + core, m)
+
+    def c_swap():
+        return copy(grad_out_hbm, g_all.at[chip], c2_send.at[0], c2_recv.at[0], ((1 - x_lo) * RING + z) * 2 + core, m)
+
+    def c_near(k):
+        slot = c_slot(1 - x_lo, 0)
+        return copy(g_all.at[slot], g_all.at[slot], c2_send.at[k], c2_recv.at[k],
                     (x_lo * RING + z_at(k)) * 2 + core, m)
 
-    def s_far(k):
-        slot = s_slot(x_lo, k)
-        return copy(s_all.at[slot], s_all.at[slot], s2_send.at[k], s2_recv.at[k],
+    def c_far(k):
+        slot = c_slot(x_lo, k)
+        return copy(g_all.at[slot], g_all.at[slot], c2_send.at[k], c2_recv.at[k],
                     ((1 - x_lo) * RING + z) * 2 + core, m)
 
-    def pass_on(row, k):
-        slot = s_slot(x_lo if row == 0 else 1 - x_lo, k)
-        return copy(s_all.at[slot], s_all.at[slot], f_send.at[row * RING + k], f_recv.at[row * RING + k], sib, m)
-
-    def passed(row, k):
-        slot = s_slot(x_lo if row == 0 else 1 - x_lo, k) + 1 - 2 * core
-        return copy(s_all.at[slot], s_all.at[slot], f_send.at[row * RING + k], f_recv.at[row * RING + k], sib, m)
+    def d_copy(k):
+        return copy(degrees_hbm, deg_all.at[chip], d_send.at[k], d_recv.at[k], chip_peer(k) * 2 + core, m)
+
+    def inv_root(q):
+        return lax.rsqrt(deg_all[q].astype(F32))
+
+    def pass_on(q):
+        r = q * 2 + core
+        return copy(s_all.at[r], s_all.at[r], f_send.at[q], f_recv.at[q], sib, m)
+
+    def passed(q):
+        r = q * 2 + 1 - core
+        return copy(s_all.at[r], s_all.at[r], f_send.at[q], f_recv.at[q], sib, m)
+
+    def project(q):
+        scaled_t = lax.dot_general(weight[...], g_all[q], (((1,), (1,)), ((), ())), preferred_element_type=F32)
+        s_all[q * 2 + core] = (scaled_t * inv_root(q)).astype(BF16)
+        pass_on(q).start()
 
     x_swap().start()
     for k in FAR + NEAR:
         x_copy(k).start()
-
-    for c in inputs[:3]:
-        c.wait()
-    inv_row = lax.rsqrt(degrees[...].astype(F32))
-    scaled_t = lax.dot_general(weight[...], grad_out[...], (((1,), (1,)), ((), ())),
-                               preferred_element_type=F32)
-    s_all[t] = (scaled_t * inv_row).astype(BF16)
-    s_swap().start()
-    for k in FAR + NEAR:
-        s_copy(k).start()
-    pass_on(0, 0).start()
-
-    for c in inputs[3:]:
+    c_swap().start()
+    for k in NEAR:
+        c_copy(k).start()
+    for c in inputs:
+        c.start()
+    for c in range(COLS // 4):
+        tile_copy(c).start()
+
+    @pl.loop(1, N_CHIP)
+    def _(k):
+        d_copy(k).start()
+
+    for c in inputs:
         c.wait()
     row_ids = lax.broadcasted_iota(jnp.int32, (N_TEAM, COLS), 0)
     slots = jnp.full((N_TEAM, COLS), SLOTS, jnp.int32)
@@ -162,8 +176,7 @@
     s_all[N_TEAM] = jnp.zeros((FEAT, BLOCK), BF16)
     for c in range(COLS):
         prod[c * HELD + SLOTS] = jnp.zeros((BLOCK, FEAT), F32)
-    inv_col = jnp.transpose(jnp.broadcast_to(inv_row, (BLOCK, BLOCK)))
-    for c in range(COLS):
+    for c in range(COLS // 4):
         tile_copy(c).wait()
     slot_copy.wait()
 
@@ -174,31 +187,36 @@
     x_swap().wait_recv()
     for k in NEAR:
         x_near(k).start()
-    s_swap().wait_recv()
-    for k in NEAR:
-        s_near(k).start()
-    pass_on(1, 0).start()
     multiply(m)
     multiply(x_slot(1 - x_hi, 0))
     for k in FAR:
         x_copy(k).wait_recv()
         x_far(k).start()
-        s_copy(k).wait_recv()
-        s_far(k).start()
-        pass_on(0, k).start()
+    c_swap().wait_recv()
+    for k in (6, 2):
+        c_copy(k).wait_recv()
+    for k in FAR:
+        c_relay(k).start()
+    for k in NEAR:
+        c_near(k).start()
     for k in FAR:
         multiply(x_slot(x_hi, k))
     for k in NEAR:
         x_copy(k).wait_recv()
         multiply(x_slot(x_hi, k))
-    for k in NEAR:
-        s_copy(k).wait_recv()
-        pass_on(0, k).start()
+
+    @pl.loop(1, N_CHIP)
+    def _(k):
+        d_copy(k).wait_recv()
+
+    project(chip)
     for k in NEAR:
         x_near(k).wait_recv()
         multiply(x_slot(1 - x_hi, k))
     for k in FAR:
         x_far(k).wait_recv()
+        c_relay(k).wait_recv()
+        c_far(k).start()
         multiply(x_slot(1 - x_hi, k))
 
     def row_sum(r):
@@ -221,11 +239,16 @@
         to_sib[q] = row_sum(q * 2 + 1 - core).astype(BF16)
         cs_copy(q).start()
 
-    def for_team(q):
+    def finish_block(q):
         mine = row_sum(q * 2 + core)
         cs_copy(q).wait_recv()
+        total = mine + from_sib[q].astype(F32)
+        q_t[q] = (jnp.transpose(total) * inv_root(q)).astype(BF16)
+        return total
+
+    def for_team(q):
         k = lax.rem(q - chip + N_CHIP, N_CHIP)
-        to_team[k] = (mine + from_sib[q].astype(F32)).astype(BF16)
+        to_team[k] = finish_block(q).astype(BF16)
         t_copy(k).start()
 
     @pl.loop(0, RING)
@@ -241,53 +264,25 @@
         for_team(x_lo * RING + dz)
 
     for_team((1 - x_lo) * RING + z)
-    mine = row_sum(t)
-    cs_copy(chip).wait_recv()
-    own_part[...] = mine + from_sib[chip].astype(F32)
-
-    for k in NEAR:
-        s_near(k).wait_recv()
-        pass_on(1, k).start()
+    own_part[...] = finish_block(chip)
+
+    for k in (7, 1):
+        c_copy(k).wait_recv()
+
+    def weight_part(row):
+        first = row * RING
+        return jnp.dot(jnp.concatenate([q_t[first + i] for i in range(RING)], axis=1),
+                       g_all[pl.ds(first, RING)].reshape(RING * BLOCK, HID), preferred_element_type=F32)
+
+    part = weight_part(x_lo)
+    for k in FAR + NEAR:
+        project(c_slot(x_lo, k))
+    project(c_slot(1 - x_lo, 0))
+    for k in NEAR:
+        c_near(k).wait_recv()
     for k in FAR:
-        s_far(k).wait_recv()
-        pass_on(1, k).start()
-
-    @pl.loop(0, RING)
-    def _(k):
-        passed(0, k).wait_recv()
-        passed(1, k).wait_recv()
-
-    def column(c):
-        picked = [s_all[jnp.where(s < count[0, c], row_of[s, c], N_TEAM)] for s in range(SLOTS)]
-        return jnp.dot(jnp.concatenate(picked, axis=1), tiles[c], preferred_element_type=F32)
-
-    def b_copy(k):
-        return copy(to_member.at[k], from_member.at[k], b_send.at[k], b_recv.at[k], t, member_peer(k))
-
-    def for_member(c):
-        k = lax.rem(c - m + N_MEMBER, N_MEMBER)
-        to_member[k] = column(c).astype(BF16)
-        b_copy(k).start()
-
-    @pl.loop(0, RING - 1)
-    def _(i):
-        dy = y_at(outward(i))
-        for_member((1 - x_hi) * RING + dy)
-        for_member(x_hi * RING + dy)
-
-    for_member((1 - x_hi) * RING + y)
-    own_col = column(m)
-
-    @pl.loop(1, N_CHIP)
-    def _(k):
-        t_copy(k).wait_recv()
-
-    summed = own_part[...]
-    for k in range(1, N_CHIP):
-        summed = summed + from_team[k].astype(F32)
-    aggregate = (summed * inv_col).astype(BF16)
-    part = lax.dot_general(aggregate, grad_out[...], (((0,), (0,)), ((), ())),
-                           preferred_element_type=F32).reshape(8, SLAB, HID)
+        c_far(k).wait_recv()
+    part = (part + weight_part(1 - x_lo)).reshape(8, SLAB, HID)
     gw_part[...] = part
     slab_out[...] = part.astype(BF16)
 
@@ -298,7 +293,8 @@
     for j in (7, 6, 5, 4, 3, 2, 1):
         g_copy(j).start()
 
-    out[...] = jnp.dot(aggregate, weight[...], preferred_element_type=F32).astype(BF16)
+    for k in FAR + NEAR:
+        project(c_slot(1 - x_lo, k))
 
     for j in range(1, 8):
         g_copy(j).wait_recv()
@@ -316,13 +312,39 @@
     for k in FAR + NEAR:
         y_copy(k).start()
 
-    @pl.loop(1, N_MEMBER)
-    def _(k):
-        b_copy(k).wait_recv()
-
-    for k in range(1, N_MEMBER):
-        own_col = own_col + from_member[k].astype(F32)
-    grad_feats[...] = jnp.transpose(own_col)
+    @pl.loop(0, N_CHIP)
+    def _(q):
+        passed(q).wait_recv()
+
+    def column(c):
+        picked = [s_all[jnp.where(s < count[0, c], row_of[s, c], N_TEAM)] for s in range(SLOTS)]
+        return jnp.dot(jnp.concatenate(picked, axis=1), tiles[c], preferred_element_type=F32)
+
+    def bx_copy(i):
+        return copy(to_bx.at[i], from_bx.at[i], bx_send.at[i], bx_recv.at[i], t, (1 - x_hi) * RING + y)
+
+    def b_copy(k):
+        return copy(to_member.at[k], from_member.at[k], b_send.at[k], b_recv.at[k], t, x_hi * RING + y_at(k))
+
+    @pl.loop(0, RING)
+    def _(i):
+        dy = y_at(outward(i))
+        to_bx[dy] = column((1 - x_hi) * RING + dy).astype(BF16)
+        bx_copy(dy).start()
+
+    @pl.loop(0, RING)
+    def _(i):
+        dy = y_at(outward(i))
+        held_b[dy] = column(x_hi * RING + dy)
+
+    def for_member(i):
+        k = outward(i)
+        dy = y_at(k)
+        bx_copy(dy).wait_recv()
+        to_member[k] = (held_b[dy] + from_bx[dy].astype(F32)).astype(BF16)
+        b_copy(k).start()
+
+    pl.loop(0, SPLIT)(for_member)
 
     for k in range(1, RING):
         y_copy(k).wait_recv()
@@ -331,6 +353,19 @@
     slab_y[...] = part.astype(BF16)
     for k in FAR + NEAR:
         z_copy(k).start()
+    pl.loop(SPLIT, RING - 1)(for_member)
+
+    @pl.loop(1, N_CHIP)
+    def _(k):
+        t_copy(k).wait_recv()
+
+    summed = own_part[...]
+    for k in range(1, N_CHIP):
+        summed = summed + from_team[k].astype(F32)
+    inv_col = jnp.transpose(jnp.broadcast_to(inv_root(chip), (BLOCK, BLOCK)))
+    aggregate = (summed * inv_col).astype(BF16)
+    out[...] = jnp.dot(aggregate, weight[...], preferred_element_type=F32).astype(BF16)
+
     for k in range(1, RING):
         z_copy(k).wait_recv()
     part = slab_y[...].astype(F32)
@@ -345,33 +380,46 @@
     for j in (7, 6, 5, 4, 3, 2, 1):
         a_copy(j).start()
 
+    bx_copy(y).wait_recv()
+    own_col = held_b[y] + from_bx[y].astype(F32)
+    for k in FAR + NEAR:
+        b_copy(k).wait_recv()
+        own_col = own_col + from_member[k].astype(F32)
+    grad_feats[...] = jnp.transpose(own_col)
+
     @pl.loop(1, N_MEMBER)
     def _(k):
         t_copy(k).wait_send()
+        d_copy(k).wait_send()
+
+    @pl.loop(0, N_CHIP)
+    def _(k):
+        cs_copy(k).wait_send()
+
+    @pl.loop(0, RING)
+    def _(k):
+        bx_copy(k).wait_send()
+
+    @pl.loop(1, RING)
+    def _(k):
         b_copy(k).wait_send()
-
-    @pl.loop(0, N_CHIP)
-    def _(k):
-        cs_copy(k).wait_send()
-
-    @pl.loop(1, RING)
-    def _(k):
         x_copy(k).wait_send()
-        s_copy(k).wait_send()
 
     x_swap().wait_send()
-    s_swap().wait_send()
+    c_swap().wait_send()
     for k in NEAR:
         x_near(k).wait_send()
-        s_near(k).wait_send()
+        c_near(k).wait_send()
+        c_copy(k).wait_send()
     for k in FAR:
         x_far(k).wait_send()
-        s_far(k).wait_send()
+        c_far(k).wait_send()
+        c_relay(k).wait_send()
 
     @pl.loop(0, RING)
     def _(k):
-        pass_on(0, k).wait_send()
-        pass_on(1, k).wait_send()
+        pass_on(k).wait_send()
+        pass_on(RING + k).wait_send()
 
     for j in range(1, 8):
         g_copy(j).wait_send()
@@ -419,9 +467,10 @@
             pltpu.VMEM((N_TEAM, COLS), jnp.int32),
             pltpu.VMEM((SLOTS, COLS), jnp.int32),
             pltpu.VMEM((1, COLS), jnp.int32),
-            pltpu.VMEM((1, BLOCK), jnp.int32),
+            pltpu.VMEM((N_CHIP, 1, BLOCK), jnp.int32),
             pltpu.VMEM((FEAT, HID), BF16),
-            pltpu.VMEM((BLOCK, HID), BF16),
+            pltpu.VMEM((N_CHIP, BLOCK, HID), BF16),
+            pltpu.VMEM((N_CHIP,) + block, BF16),
             pltpu.VMEM((COLS, SLOTS * BLOCK, BLOCK), BF16),
             pltpu.VMEM((COLS,) + block, BF16),
             pltpu.VMEM((N_TEAM + 1,) + block, BF16),
@@ -431,8 +480,11 @@
             pltpu.VMEM(block, F32),
             pltpu.VMEM((N_CHIP,) + block, BF16),
             pltpu.VMEM((N_CHIP,) + block, BF16),
-            pltpu.VMEM((N_MEMBER,) + block, BF16),
-            pltpu.VMEM((N_MEMBER,) + block, BF16),
+            pltpu.VMEM((RING,) + block, BF16),
+            pltpu.VMEM((RING,) + block, BF16),
+            pltpu.VMEM((RING,) + block, F32),
+            pltpu.VMEM((RING,) + block, BF16),
+            pltpu.VMEM((RING,) + block, BF16),
             pltpu.VMEM((8, SLAB, HID), F32),
             pltpu.VMEM((8, SLAB, HID), BF16),
             pltpu.VMEM((8, SLAB, HID), BF16),
@@ -440,11 +492,11 @@
             pltpu.VMEM((8, SLAB, HID), BF16),
             pltpu.VMEM((SLAB, HID), BF16),
             pltpu.VMEM((8, SLAB, HID), BF16),
-            dma((8,)), dma, dma((COLS,)),
+            dma((8,)), dma, dma((COLS // 4,)),
             dma((8,)), dma((8,)), dma((8,)), dma((8,)), dma((8,)), dma((8,)), dma((8,)), dma((8,)),
-            dma((16,)), dma((16,)), dma((16,)), dma((16,)),
-            dma((16,)), dma((16,)), dma((16,)), dma((16,)), dma((8,)), dma((8,)), dma((8,)), dma((8,)),
-            dma((8,)), dma((8,)), dma((8,)), dma((8,)),
+            dma((16,)), dma((16,)), dma((16,)), dma((16,)), dma((16,)), dma((16,)),
+            dma((16,)), dma((16,)), dma((8,)), dma((8,)), dma((8,)), dma((8,)), dma((8,)), dma((8,)),
+            dma((8,)), dma((8,)), dma((8,)), dma((8,)), dma((8,)), dma((8,)),
         ],
         compiler_params=pltpu.CompilerParams(
             collective_id=0, has_side_effects=True, vmem_limit_bytes=60 * 1024 * 1024),

time: 66.1 us -> 61.5 us (0.930)
  Pallas kernels: 65.3 us -> 60.7 us
    pallas_call x1, Pallas kernels: 63.7 us -> 59.1 us  [per_device(): pl.pallas_call(kernel, out_shape=out_shape, in_specs=[hbm] * 7, out_specs...]
where the time goes in v3:
time: 61.5 us; the launch traced here: 61.4 us
  Pallas kernels  60.7 us (99%)
  between operations  0.64 us (1%)
    pallas_call x1, Pallas kernels, per_device(): pl.pallas_call(kernel, out_shape=out_shape, in_specs=[hbm] * 7, out_specs...  59.1 us
    pallas_call x1, Pallas kernels, per_device(): pl.pallas_call(place, out_shape=out_shape, in_specs=[hbm] * 3, out_specs=...  1.64 us

profile of v3, /device:TPU:1, one launch (start us, length us, event | category | flops | bytes accessed | tf_op | source)
XLA Modules:
  0.0 61.4 jit_solution(6332081578043968479)
XLA Ops:
  0.6 59.1 %shard_map.94 = (bf16[128,256]{1,0:T(8,128)(2,1)}, f32[8,16,256]{2,1,0:T(8,128)}, f32[128,128]{1,0:T(8,128)}) custom-call(s32[8,16]{1,0:T(8,128)} %bitcast.8, s32[1,16]{1,0:T(1,128)} %bitcast.9, bf16[128,128]{1,0:T(8,128)(2,1)} %feats_hbm.1, bf16[16,1024,128]{2,1,0:T(8,128)(2,1)} %bitcast.7, s32[1,128]{1,0:T(1,128)} %bitcast.10, ...), custom_call_target="tpu_custom_call" | custom-call | tf_op jit(solution)/shard_map/pallas_call | solution.py:458
  59.7 1.6 %shard_map.95 = (bf16[128,256]{1,0:T(8,128)(2,1)}, f32[8,16,256]{2,1,0:T(8,128)}, f32[128,128]{1,0:T(8,128)}) custom-call(bf16[128,256]{1,0:T(8,128)(2,1)} %get-tuple-element.9.out, f32[8,16,256]{2,1,0:T(8,128)} %get-tuple-element.10.grad_weight, f32[128,128]{1,0:T(8,128)} %get-tuple-element.11.grad_feats), custom_call_target="tpu_custom_call" | custom-call | tf_op jit(solution)/shard_map/pallas_call | solution.py:508

commit v4 on v3

--- a/solution.py
+++ b/solution.py
@@ -15,13 +15,13 @@
 HELD = SLOTS + 1
 SLAB = BLOCK // 8
 FAR, NEAR = (4, 3, 5), (6, 2, 7, 1)
-SPLIT = 4
+SPLIT = 2
 
 
 def kernel(row_hbm, count_hbm, feats_hbm, tiles_hbm, degrees_hbm, weight_hbm, grad_out_hbm,
            out, grad_weight, grad_feats,
            slot_of, row_of, count, slot_vec, row_vec, count_vec, deg_all, weight, g_all, q_t,
-           tiles, x_all, s_all, prod, from_sib, to_sib, own_part, to_team, from_team,
+           tiles, x_all, s_all, prod, part_sum, from_sib, to_sib, own_part, to_team, from_team,
            to_bx, from_bx, held_b, to_member, from_member, gw_part, slab_out, slab_in, slab, y_in, slab_y, z_in,
            in_sem, slot_sem, tile_sem, x_send, x_recv, x2_send, x2_recv, c_send, c_recv, c2_send, c2_recv, d_send, d_recv,
            f_send, f_recv, cs_send, cs_recv,
@@ -144,10 +144,14 @@
         r = q * 2 + 1 - core
         return copy(s_all.at[r], s_all.at[r], f_send.at[q], f_recv.at[q], sib, m)
 
-    def project(q):
-        scaled_t = lax.dot_general(weight[...], g_all[q], (((1,), (1,)), ((), ())), preferred_element_type=F32)
-        s_all[q * 2 + core] = (scaled_t * inv_root(q)).astype(BF16)
-        pass_on(q).start()
+    def project(row):
+        first = row * RING
+        scaled_t = lax.dot_general(weight[...], g_all[pl.ds(first, RING)].reshape(RING * BLOCK, HID),
+                                   (((1,), (1,)), ((), ())), preferred_element_type=F32)
+        for i in range(RING):
+            q = first + i
+            s_all[q * 2 + core] = (scaled_t[:, i * BLOCK:(i + 1) * BLOCK] * inv_root(q)).astype(BF16)
+            pass_on(q).start()
 
     x_swap().start()
     for k in FAR + NEAR:
@@ -209,19 +213,30 @@
     def _(k):
         d_copy(k).wait_recv()
 
-    project(chip)
+    early = [x_slot(x_hi, k) for k in range(RING)] + [x_slot(1 - x_hi, 0)]
+
+    @pl.loop(0, N_TEAM)
+    def _(r):
+        total = prod[early[0] * HELD + slot_of[r, early[0]]]
+        for c in early[1:]:
+            total = total + prod[c * HELD + slot_of[r, c]]
+        part_sum[r] = total
+
     for k in NEAR:
         x_near(k).wait_recv()
         multiply(x_slot(1 - x_hi, k))
     for k in FAR:
-        x_far(k).wait_recv()
         c_relay(k).wait_recv()
         c_far(k).start()
+    for k in FAR:
+        x_far(k).wait_recv()
         multiply(x_slot(1 - x_hi, k))
 
+    late = [x_slot(1 - x_hi, k) for k in range(1, RING)]
+
     def row_sum(r):
-        total = prod[slot_of[r, 0]]
-        for c in range(1, COLS):
+        total = part_sum[r]
+        for c in late:
             total = total + prod[c * HELD + slot_of[r, c]]
         return total
 
@@ -275,9 +290,7 @@
                        g_all[pl.ds(first, RING)].reshape(RING * BLOCK, HID), preferred_element_type=F32)
 
     part = weight_part(x_lo)
-    for k in FAR + NEAR:
-        project(c_slot(x_lo, k))
-    project(c_slot(1 - x_lo, 0))
+    project(x_lo)
     for k in NEAR:
         c_near(k).wait_recv()
     for k in FAR:
@@ -293,8 +306,27 @@
     for j in (7, 6, 5, 4, 3, 2, 1):
         g_copy(j).start()
 
-    for k in FAR + NEAR:
-        project(c_slot(1 - x_lo, k))
+    project(1 - x_lo)
+
+    @pl.loop(0, N_CHIP)
+    def _(q):
+        passed(q).wait_recv()
+
+    def column(c):
+        picked = [s_all[jnp.where(s < count[0, c], row_of[s, c], N_TEAM)] for s in range(SLOTS)]
+        return jnp.dot(jnp.concatenate(picked, axis=1), tiles[c], preferred_element_type=F32)
+
+    def bx_copy(i):
+        return copy(to_bx.at[i], from_bx.at[i], bx_send.at[i], bx_recv.at[i], t, (1 - x_hi) * RING + y)
+
+    def b_copy(k):
+        return copy(to_member.at[k], from_member.at[k], b_send.at[k], b_recv.at[k], t, x_hi * RING + y_at(k))
+
+    @pl.loop(0, RING)
+    def _(i):
+        dy = y_at(outward(i))
+        to_bx[dy] = column((1 - x_hi) * RING + dy).astype(BF16)
+        bx_copy(dy).start()
 
     for j in range(1, 8):
         g_copy(j).wait_recv()
@@ -311,26 +343,6 @@
 
     for k in FAR + NEAR:
         y_copy(k).start()
-
-    @pl.loop(0, N_CHIP)
-    def _(q):
-        passed(q).wait_recv()
-
-    def column(c):
-        picked = [s_all[jnp.where(s < count[0, c], row_of[s, c], N_TEAM)] for s in range(SLOTS)]
-        return jnp.dot(jnp.concatenate(picked, axis=1), tiles[c], preferred_element_type=F32)
-
-    def bx_copy(i):
-        return copy(to_bx.at[i], from_bx.at[i], bx_send.at[i], bx_recv.at[i], t, (1 - x_hi) * RING + y)
-
-    def b_copy(k):
-        return copy(to_member.at[k], from_member.at[k], b_send.at[k], b_recv.at[k], t, x_hi * RING + y_at(k))
-
-    @pl.loop(0, RING)
-    def _(i):
-        dy = y_at(outward(i))
-        to_bx[dy] = column((1 - x_hi) * RING + dy).astype(BF16)
-        bx_copy(dy).start()
 
     @pl.loop(0, RING)
     def _(i):
@@ -475,6 +487,7 @@
             pltpu.VMEM((COLS,) + block, BF16),
             pltpu.VMEM((N_TEAM + 1,) + block, BF16),
             pltpu.VMEM((COLS * HELD,) + block, F32),
+            pltpu.VMEM((N_TEAM,) + block, F32),
             pltpu.VMEM((N_CHIP,) + block, BF16),
             pltpu.VMEM((N_CHIP,) + block, BF16),
             pltpu.VMEM(block, F32),

time: 61.5 us -> 57.8 us (0.940)
  Pallas kernels: 60.7 us -> 57 us
    pallas_call x1, Pallas kernels: 59.1 us -> 55.4 us  [per_device(): pl.pallas_call(kernel, out_shape=out_shape, in_specs=[hbm] * 7, out_specs...]
where the time goes in v4:
time: 57.8 us; the launch traced here: 57.7 us
  Pallas kernels  57 us (99%)
  between operations  0.64 us (1%)
    pallas_call x1, Pallas kernels, per_device(): pl.pallas_call(kernel, out_shape=out_shape, in_specs=[hbm] * 7, out_specs...  55.4 us
    pallas_call x1, Pallas kernels, per_device(): pl.pallas_call(place, out_shape=out_shape, in_specs=[hbm] * 3, out_specs=...  1.64 us

profile of v4, /device:TPU:1, one launch (start us, length us, event | category | flops | bytes accessed | tf_op | source)
XLA Modules:
  0.0 57.7 jit_solution(4291662445404924932)
XLA Ops:
  0.6 55.4 %shard_map.94 = (bf16[128,256]{1,0:T(8,128)(2,1)}, f32[8,16,256]{2,1,0:T(8,128)}, f32[128,128]{1,0:T(8,128)}) custom-call(s32[8,16]{1,0:T(8,128)} %bitcast.8, s32[1,16]{1,0:T(1,128)} %bitcast.9, bf16[128,128]{1,0:T(8,128)(2,1)} %feats_hbm.1, bf16[16,1024,128]{2,1,0:T(8,128)(2,1)} %bitcast.7, s32[1,128]{1,0:T(1,128)} %bitcast.10, ...), custom_call_target="tpu_custom_call" | custom-call | tf_op jit(solution)/shard_map/pallas_call | solution.py:470
  56.0 1.6 %shard_map.95 = (bf16[128,256]{1,0:T(8,128)(2,1)}, f32[8,16,256]{2,1,0:T(8,128)}, f32[128,128]{1,0:T(8,128)}) custom-call(bf16[128,256]{1,0:T(8,128)(2,1)} %get-tuple-element.9.out, f32[8,16,256]{2,1,0:T(8,128)} %get-tuple-element.10.grad_weight, f32[128,128]{1,0:T(8,128)} %get-tuple-element.11.grad_feats), custom_call_target="tpu_custom_call" | custom-call | tf_op jit(solution)/shard_map/pallas_call | solution.py:521

commit v5 on v4

--- a/solution.py
+++ b/solution.py
@@ -153,12 +153,14 @@
             s_all[q * 2 + core] = (scaled_t[:, i * BLOCK:(i + 1) * BLOCK] * inv_root(q)).astype(BF16)
             pass_on(q).start()
 
+    for k in (6, 2):
+        c_copy(k).start()
     x_swap().start()
     for k in FAR + NEAR:
         x_copy(k).start()
+    for k in (7, 1):
+        c_copy(k).start()
     c_swap().start()
-    for k in NEAR:
-        c_copy(k).start()
     for c in inputs:
         c.start()
     for c in range(COLS // 4):
@@ -322,11 +324,12 @@
     def b_copy(k):
         return copy(to_member.at[k], from_member.at[k], b_send.at[k], b_recv.at[k], t, x_hi * RING + y_at(k))
 
-    @pl.loop(0, RING)
-    def _(i):
+    def for_other(i):
         dy = y_at(outward(i))
         to_bx[dy] = column((1 - x_hi) * RING + dy).astype(BF16)
         bx_copy(dy).start()
+
+    pl.loop(0, 4)(for_other)
 
     for j in range(1, 8):
         g_copy(j).wait_recv()
@@ -343,6 +346,8 @@
 
     for k in FAR + NEAR:
         y_copy(k).start()
+
+    pl.loop(4, RING)(for_other)
 
     @pl.loop(0, RING)
     def _(i):
@@ -442,17 +447,13 @@
         a_copy(j).wait_recv()
 
 
-def place(out, grad_weight, grad_feats, to_out, to_weight, to_feats, held_out, held_weight, held_feats, sem):
-    held = (held_out, held_weight, held_feats)
-    inward = [pltpu.make_async_copy(src, dst, sem.at[i]) for i, (src, dst) in enumerate(zip((out, grad_weight, grad_feats), held))]
-    outward = [pltpu.make_async_copy(src, dst, sem.at[i]) for i, (src, dst) in enumerate(zip(held, (to_out, to_weight, to_feats)))]
-    for c in inward:
+def place(out, grad_weight, grad_feats, to_out, to_weight, to_feats, sem):
+    pairs = ((out, to_out), (grad_weight, to_weight), (grad_feats, to_feats))
+    copies = [pltpu.make_async_copy(src, dst, sem.at[i]) for i, (src, dst) in enumerate(pairs)]
+    for c in copies:
         c.start()
-    for c, d in zip(inward, outward):
+    for c in copies:
         c.wait()
-        d.start()
-    for d in outward:
-        d.wait()
 
 
 def per_device(feats, tile_weights, tile_rows, slot_count, degrees, weight, grad_out):
@@ -521,9 +522,9 @@
     out, grad_weight, grad_feats = pl.pallas_call(
         place,
         out_shape=out_shape,
-        in_specs=[hbm] * 3,
+        in_specs=[vmem] * 3,
         out_specs=(hbm,) * 3,
-        scratch_shapes=[pltpu.VMEM(o.shape, o.dtype) for o in out_shape] + [dma((3,))],
+        scratch_shapes=[dma((3,))],
     )(*results)
     return out, grad_weight.reshape(BLOCK, HID), grad_feats
 

time: 57.8 us -> 57.8 us (level)
  no operation moved by 1% of the time
where the time goes in v5:
time: 57.8 us; the launch traced here: 57.7 us
  Pallas kernels  57 us (99%)
  between operations  0.64 us (1%)
    pallas_call x1, Pallas kernels, per_device(): pl.pallas_call(kernel, out_shape=out_shape, in_specs=[hbm] * 7, out_specs...  55.4 us
    pallas_call x1, Pallas kernels, per_device(): pl.pallas_call(place, out_shape=out_shape, in_specs=[vmem] * 3, out_specs...  1.65 us

profile of v5, /device:TPU:1, one launch (start us, length us, event | category | flops | bytes accessed | tf_op | source)
XLA Modules:
  0.0 57.7 jit_solution(13791469334532811310)
XLA Ops:
  0.6 55.4 %shard_map.94 = (bf16[128,256]{1,0:T(8,128)(2,1)}, f32[8,16,256]{2,1,0:T(8,128)}, f32[128,128]{1,0:T(8,128)}) custom-call(s32[8,16]{1,0:T(8,128)} %bitcast.8, s32[1,16]{1,0:T(1,128)} %bitcast.9, bf16[128,128]{1,0:T(8,128)(2,1)} %feats_hbm.1, bf16[16,1024,128]{2,1,0:T(8,128)(2,1)} %bitcast.7, s32[1,128]{1,0:T(1,128)} %bitcast.10, ...), custom_call_target="tpu_custom_call" | custom-call | tf_op jit(solution)/shard_map/pallas_call | solution.py:471
  56.0 1.7 %shard_map.95 = (bf16[128,256]{1,0:T(8,128)(2,1)}, f32[8,16,256]{2,1,0:T(8,128)}, f32[128,128]{1,0:T(8,128)}) custom-call(bf16[128,256]{1,0:T(8,128)(2,1)} %get-tuple-element.9.out, f32[8,16,256]{2,1,0:T(8,128)} %get-tuple-element.10.grad_weight, f32[128,128]{1,0:T(8,128)} %get-tuple-element.11.grad_feats), custom_call_target="tpu_custom_call" | custom-call | tf_op jit(solution)/shard_map/pallas_call | solution.py:522
